TPU v7x, 32 devices: a whole 2x2x4 slice. The times are simulated.
32 devices in a mesh: row: 8 (over y, x, core), col: 4 (over z).
Axes of the slice: x: 2, y: 2, z: 4, core: 2. Of those that a mesh axis runs over, the one named last changes fastest.
Arguments:
- x_tiles: bfloat16 [128, 8, 256, 256], P(('row', 'col')), as said below
- columns: int32 [128, 8], P(('row', 'col')), may hold values from 0 to 127, as said below
- branch: int32 [8, 2], P('row'), may hold values from 0 to 1
Outputs:
- purified: float32 [128, 8, 256, 256], P(('row', 'col'))
- occupation: float32 [8], P('row')
Inputs may be any that keep to these rules, and one draw needn't show every extreme that they name: `columns`: block rows form fragments of 16 consecutive rows, each with two halves of 8 rows. Slot 0 of a block row is the row itself; its other slots hold, in ascending order, every row of the other half of its fragment but one, so that the pattern is symmetric and no two rows of one half are coupled. `x_tiles`: every tile of the pattern is the transpose of its mirror tile, and diagonal tiles are symmetric.
All inputs are finite; a program needn't handle non-finite values.
Results may differ from a plain program's by a relative error of at most 0.0028.
Values may be sent and summed in bfloat16 or wider, within the bound.
A program may use at most 128 MiB of HBM per device.

v0:
```python
import functools

import jax
import jax.numpy as jnp
from jax import lax
from jax.experimental import pallas as pl
from jax.experimental.pallas import tpu as pltpu
from jax.sharding import PartitionSpec as P

MESH = pl.DeviceIdType.MESH
HEAD = 16
WINDOW = 4
AHEAD = 2
NN = (((1,), (0,)), ((), ()))
NT = (((1,), (1,)), ((), ()))


def mm(a, b, dims=NN):
    return lax.dot_general(a, b, dims, preferred_element_type=jnp.float32)


def purify_kernel(
    n, cols_hbm, branch_hbm, x_hbm, out_ref, occ_ref,
    cols_ref, branch_ref, x, d1, send, recv, gath, trace, load_sem, send_sem, recv_sem, pass_sem, tsend_sem, trecv_sem,
):
    rows, slots, size = x.shape[0], x.shape[1], x.shape[2]
    half_tile = size // 2
    h = n // 2
    half_rows = rows * h
    me = lax.axis_index("col")
    upper = (me >= h).astype(jnp.int32)
    mine = me - upper * h
    first = upper * h
    mirror = n - 1 - me
    theirs = h - 1 - mine

    load_diag = pltpu.make_async_copy(x_hbm.at[:, 0:1], x.at[:, 0:1], load_sem.at[0])
    load_rest = pltpu.make_async_copy(x_hbm.at[:, 1:slots], x.at[:, 1:slots], load_sem.at[1])
    load_diag.start()
    load_cols = pltpu.make_async_copy(cols_hbm, cols_ref, load_sem.at[2])
    load_branch = pltpu.make_async_copy(branch_hbm, branch_ref, load_sem.at[3])
    load_cols.start()
    load_branch.start()
    load_rest.start()

    barrier = pltpu.get_barrier_semaphore()
    for k in range(1, n):
        pl.semaphore_signal(barrier, inc=1, device_id={"col": lax.rem(me + k, n)}, device_id_type=MESH)

    load_cols.wait()
    load_branch.wait()
    signs = [(2 * branch_ref[0, step] - 1).astype(jnp.float32) for step in range(2)]
    ri = lax.broadcasted_iota(jnp.int32, (half_tile, half_tile), 0)
    ci = lax.broadcasted_iota(jnp.int32, (half_tile, half_tile), 1)
    head_row = lax.broadcasted_iota(jnp.int32, (HEAD, half_tile), 0)
    eye = (
        lax.broadcasted_iota(jnp.int32, (size, size), 0) == lax.broadcasted_iota(jnp.int32, (size, size), 1)
    )

    def piece(k):
        step, q = divmod(k, 2 * rows)
        at, end = HEAD + q * half_tile, HEAD + (q + 1) * half_tile
        at = 0 if q == 0 else at
        return step, q, pl.ds(at, end - at)

    def pack(tile, step, t, head):
        a11 = tile[:half_tile, :half_tile]
        a22 = tile[half_tile:, half_tile:]
        at = pl.multiple_of(HEAD + t * size, HEAD)
        send[step, pl.ds(at, half_tile), :] = jnp.where(ri <= ci, a11, a22).astype(jnp.bfloat16)
        send[step, pl.ds(at + half_tile, half_tile), :] = tile[:half_tile, half_tile:].astype(jnp.bfloat16)
        corner = jnp.sum(jnp.where(ri == ci, a22, 0.0), axis=0, keepdims=True)
        return head + jnp.where(head_row == t, corner, 0.0)

    def own_copy(k):
        step, q, span = piece(k)
        return pltpu.make_async_remote_copy(
            src_ref=send.at[step, span],
            dst_ref=recv.at[step, mine, span],
            send_sem=send_sem.at[step, q],
            recv_sem=recv_sem.at[step, mine, q],
            device_id={"col": mirror},
            device_id_type=MESH,
        )

    def pass_copy(k, j):
        step, q, span = piece(k)
        return pltpu.make_async_remote_copy(
            src_ref=recv.at[step, theirs, span],
            dst_ref=recv.at[step, theirs, span],
            send_sem=pass_sem.at[step, j, q],
            recv_sem=recv_sem.at[step, theirs, q],
            device_id={"col": first + lax.rem(mine + j, h)},
            device_id_type=MESH,
        )

    def landing(k, j):
        step, q, span = piece(k)
        sibling = lax.rem(mine + h - j, h)
        source = h - 1 - sibling
        return pltpu.make_async_remote_copy(
            src_ref=recv.at[step, source, span],
            dst_ref=recv.at[step, source, span],
            send_sem=pass_sem.at[step, j, q],
            recv_sem=recv_sem.at[step, source, q],
            device_id={"col": mirror},
            device_id_type=MESH,
        )

    pieces = 4 * rows
    begun = [0]
    direct = [0]
    sent = [0]

    def pump(upto):
        while begun[0] < min(upto, pieces):
            own_copy(begun[0]).start()
            begun[0] += 1

    def relay(upto):
        while direct[0] < min(upto, pieces):
            k = direct[0]
            if begun[0] < pieces:
                own_copy(k).wait_send()
                sent[0] += 1
                pump(k + 1 + WINDOW)
            landing(k, 0).wait_recv()
            for j in range(1, h):
                pass_copy(k, j).start()
            direct[0] += 1

    def arrive(k):
        relay(k + 1 + AHEAD)
        for j in range(1, h):
            landing(k, j).wait_recv()

    def unpack(step, t):
        for r in range(h):
            at = HEAD + t * size
            mixed = recv[step, r, pl.ds(at, half_tile), :].astype(jnp.float32)
            cross = recv[step, r, pl.ds(at + half_tile, half_tile), :]
            head = recv[step, r, 0:HEAD, :].astype(jnp.float32)
            corner = jnp.sum(jnp.where(head_row == t, head, 0.0), axis=0, keepdims=True)
            turned = mixed.T
            a11 = jnp.where(ri <= ci, mixed, turned)
            a22 = jnp.where(ri > ci, mixed, jnp.where(ri == ci, corner, turned))
            g = r * rows + t
            gath[step, g, 0:half_tile, 0:half_tile] = a11.astype(jnp.bfloat16)
            gath[step, g, half_tile:, half_tile:] = a22.astype(jnp.bfloat16)
            gath[step, g, 0:half_tile, half_tile:] = cross
            gath[step, g, half_tile:, 0:half_tile] = cross.astype(jnp.float32).T.astype(jnp.bfloat16)

    def ready(t):
        return [
            s for s in range(slots - 1)
            if max(s % rows, (s + 1) % rows) == t
        ]

    def other(step, i, s):
        first = lax.rem(cols_ref[i, s + 1], half_rows) == s
        return lax.select(first, gath[step, s], gath[step, s + 1])

    load_diag.wait()
    head = jnp.zeros((HEAD, half_tile), jnp.float32)
    for t in range(rows):
        head = pack(x[t, 0].astype(jnp.float32), 0, t, head)
    send[0, 0:HEAD, :] = head.astype(jnp.bfloat16)
    pl.semaphore_wait(barrier, n - 1)
    pump(min(WINDOW, 2 * rows))
    load_rest.wait()

    def first_diagonal(i, head):
        total = mm(x[i, 0], x[i, 0], NT)
        for s in range(1, slots):
            total += mm(x[i, s], x[i, s], NT)
        new = x[i, 0].astype(jnp.float32) + signs[0] * (total - jnp.where(eye, 0.25, 0.0))
        out_ref[i, 0] = new
        d1[i, 0] = new.astype(jnp.bfloat16)
        return pack(new, 1, i, head)

    def first_local(i, carry):
        for s in range(1, slots):
            out_ref[i, s] = x[i, s].astype(jnp.float32) + signs[0] * mm(x[i, 0], x[i, s])
        return carry

    for t in range(rows):
        if t == 0:
            head = lax.fori_loop(0, rows, first_diagonal, jnp.zeros((HEAD, half_tile), jnp.float32))
            send[1, 0:HEAD, :] = head.astype(jnp.bfloat16)
        arrive(2 * t)
        arrive(2 * t + 1)
        if t == 0:
            lax.fori_loop(0, rows, first_local, 0, unroll=True)
        unpack(0, t)
        todo = ready(t)

        def first_partner(i, carry):
            for s in todo:
                new = out_ref[i, s + 1] + signs[0] * mm(x[i, s + 1], other(0, i, s))
                low = new.astype(jnp.bfloat16)
                d1[i, s + 1] = low
                out_ref[i, s + 1] = new + signs[1] * mm(d1[i, 0], low)
            return carry

        if todo:
            lax.fori_loop(0, rows, first_partner, 0, unroll=True)

    arrive(2 * rows)
    arrive(2 * rows + 1)
    unpack(1, 0)

    def second_diagonal(i, carry):
        total = mm(d1[i, 0], d1[i, 0], NT)
        for s in range(1, slots):
            total += mm(d1[i, s], d1[i, s], NT)
        new = out_ref[i, 0] + signs[1] * (total - jnp.where(eye, 0.25, 0.0))
        out_ref[i, 0] = new
        on_diag = jnp.where(eye, new, 0.0)
        return carry + jnp.sum(jnp.sum(on_diag.reshape(size // 8, 8, 2, half_tile), axis=0), axis=1)

    lanes = lax.fori_loop(0, rows, second_diagonal, jnp.zeros((8, half_tile), jnp.float32))
    trace[me] = lanes

    def trace_copy(k):
        return pltpu.make_async_remote_copy(
            src_ref=trace.at[me],
            dst_ref=trace.at[me],
            send_sem=tsend_sem.at[k],
            recv_sem=trecv_sem.at[k],
            device_id={"col": lax.rem(me + k, n)},
            device_id_type=MESH,
        )

    def trace_landing(k):
        source = lax.rem(me + n - k, n)
        return pltpu.make_async_remote_copy(
            src_ref=trace.at[source],
            dst_ref=trace.at[source],
            send_sem=tsend_sem.at[k],
            recv_sem=trecv_sem.at[k],
            device_id={"col": lax.rem(me + k, n)},
            device_id_type=MESH,
        )

    for k in range(1, n):
        trace_copy(k).start()

    for t in range(rows):
        if t > 0:
            arrive(2 * (rows + t))
            arrive(2 * (rows + t) + 1)
            unpack(1, t)
        todo = ready(t)

        def second_partner(i, carry):
            for s in todo:
                out_ref[i, s + 1] = out_ref[i, s + 1] + signs[1] * mm(d1[i, s + 1], other(1, i, s))
            return carry

        if todo:
            lax.fori_loop(0, rows, second_partner, 0, unroll=True)

    for k in range(1, n):
        trace_landing(k).wait_recv()
        trace_copy(k).wait_send()
    total = trace[0]
    for k in range(1, n):
        total = total + trace[k]
    scale = 1.0 / (rows * n * size)
    occ_ref[...] = jnp.broadcast_to(jnp.sum(total, keepdims=True) * scale + 0.5, occ_ref.shape)

    for k in range(sent[0], pieces):
        own_copy(k).wait_send()

    for k in range(pieces):
        for j in range(1, h):
            pass_copy(k, j).wait_send()


def write_kernel(held, occ_ref, out_hbm, occ_out, sem):
    rows, slots = held.shape[0], held.shape[1]

    def part(i, j):
        span = pl.ds(2 * j, 2)
        return pltpu.make_async_copy(held.at[i, span], out_hbm.at[i, span], sem.at[i, j])

    for i in range(rows):
        for j in range(slots // 2):
            part(i, j).start()
    occ_out[...] = occ_ref[0, 0:1]
    for i in range(rows):
        for j in range(slots // 2):
            part(i, j).wait()


def shards(n, x_tiles, columns, branch):
    rows, slots, size = x_tiles.shape[0], x_tiles.shape[1], x_tiles.shape[2]
    h = n // 2
    length = HEAD + rows * size
    vmem = pl.BlockSpec(memory_space=pltpu.VMEM)
    hbm = pl.BlockSpec(memory_space=pltpu.HBM)
    flops = 2 * size**3 * rows * (slots * 2 + (slots - 1) * 4)
    held, occ = pl.pallas_call(
        functools.partial(purify_kernel, n),
        out_shape=(
            pltpu.VMEM(x_tiles.shape, jnp.float32),
            pltpu.VMEM((8, 128), jnp.float32),
        ),
        in_specs=[hbm, hbm, hbm],
        out_specs=(vmem, vmem),
        scratch_shapes=[
            pltpu.SMEM(columns.shape, jnp.int32),
            pltpu.SMEM(branch.shape, jnp.int32),
            pltpu.VMEM((rows, slots, size, size), jnp.bfloat16),
            pltpu.VMEM((rows, slots, size, size), jnp.bfloat16),
            pltpu.VMEM((2, length, size // 2), jnp.bfloat16),
            pltpu.VMEM((2, h, length, size // 2), jnp.bfloat16),
            pltpu.VMEM((2, h * rows, size, size), jnp.bfloat16),
            pltpu.VMEM((n, 8, size // 2), jnp.float32),
            pltpu.SemaphoreType.DMA((4,)),
            pltpu.SemaphoreType.DMA((2, 2 * rows)),
            pltpu.SemaphoreType.DMA((2, h, 2 * rows)),
            pltpu.SemaphoreType.DMA((2, h, 2 * rows)),
            pltpu.SemaphoreType.DMA((n,)),
            pltpu.SemaphoreType.DMA((n,)),
        ],
        compiler_params=pltpu.CompilerParams(
            collective_id=0, has_side_effects=True, vmem_limit_bytes=40 * 2**20
        ),
        cost_estimate=pl.CostEstimate(flops=flops, bytes_accessed=3 * x_tiles.size * 2, transcendentals=0),
        name="purify",
    )(*[pltpu.with_memory_space_constraint(a, pltpu.HBM) for a in (columns, branch, x_tiles)])
    return pl.pallas_call(
        write_kernel,
        out_shape=(
            jax.ShapeDtypeStruct(x_tiles.shape, jnp.float32),
            jax.ShapeDtypeStruct((1,), jnp.float32),
        ),
        in_specs=[vmem, vmem],
        out_specs=(hbm, vmem),
        scratch_shapes=[pltpu.SemaphoreType.DMA((rows, slots // 2))],
        compiler_params=pltpu.CompilerParams(vmem_limit_bytes=4 * 2**20),
        cost_estimate=pl.CostEstimate(flops=0, bytes_accessed=x_tiles.size * 4, transcendentals=0),
        name="write",
    )(
        pltpu.with_memory_space_constraint(held, pltpu.VMEM),
        pltpu.with_memory_space_constraint(occ, pltpu.VMEM),
    )


def solution(mesh):
    placed = (P(("row", "col"), None, None, None), P(("row", "col"), None), P("row", None))
    return jax.shard_map(
        functools.partial(shards, mesh.shape["col"]),
        mesh=mesh,
        in_specs=placed,
        out_specs=(P(("row", "col"), None, None, None), P("row")),
        check_vma=False,
    )
```

profile of v0, /device:TPU:0, one launch (start us, length us, event | category | flops | bytes accessed | tf_op | source)
XLA Modules:
  0.0 41.7 jit_solution(14096589090160148512)
XLA Ops:
  0.6 37.1 %purify.1 = (f32[4,8,256,256]{3,2,1,0:T(8,128)S(1)}, f32[8,128]{1,0:T(8,128)S(1)}) custom-call(s32[4,8]{1,0:T(4,128)} %cols_hbm.1, s32[1,2]{1,0:T(1,128)} %branch_hbm.1, bf16[4,8,256,256]{3,2,1,0:T(8,128)(2,1)} %x_hbm.1), custom_call_target="tpu_custom_call" | custom-call | flops 5905580032 | bytes 12582912 | tf_op jit(solution)/shard_map/purify/pallas_call | solution.py:303
  37.8 3.9 %write.1 = (f32[4,8,256,256]{3,2,1,0:T(8,128)}, f32[1]{0:T(128)}) custom-call(f32[4,8,256,256]{3,2,1,0:T(8,128)S(1)} %get-tuple-element.4.held, f32[8,128]{1,0:T(8,128)S(1)} %get-tuple-element.5.occ_ref), custom_call_target="tpu_custom_call" | custom-call | bytes 8388608 | tf_op jit(solution)/shard_map/write/pallas_call | solution.py:333
where the time goes:
time: 41.8 us; the launch traced here: 41.7 us
  Pallas kernels  41 us (98%)
  between operations  0.64 us (2%)
    pallas_call x1, Pallas kernels, shards(): pl.pallas_call(functools.partial(purify_kernel, n), out_shape=(pltpu.VMEM...  37.1 us
    pallas_call x1, Pallas kernels, shards(): pl.pallas_call(write_kernel, out_shape=(jax.ShapeDtypeStruct(x_tiles.shap...  3.93 us

commit v1 on v0

--- a/solution.py
+++ b/solution.py
@@ -9,7 +9,7 @@
 
 MESH = pl.DeviceIdType.MESH
 HEAD = 16
-WINDOW = 4
+WINDOW = 8
 AHEAD = 2
 NN = (((1,), (0,)), ((), ()))
 NT = (((1,), (1,)), ((), ()))
@@ -112,18 +112,20 @@
     direct = [0]
     sent = [0]
 
+    limit = [2 * rows]
+
     def pump(upto):
-        while begun[0] < min(upto, pieces):
+        while begun[0] < min(upto, limit[0]):
+            if begun[0] >= WINDOW:
+                own_copy(sent[0]).wait_send()
+                sent[0] += 1
             own_copy(begun[0]).start()
             begun[0] += 1
 
     def relay(upto):
         while direct[0] < min(upto, pieces):
             k = direct[0]
-            if begun[0] < pieces:
-                own_copy(k).wait_send()
-                sent[0] += 1
-                pump(k + 1 + WINDOW)
+            pump(k + 1 + WINDOW)
             landing(k, 0).wait_recv()
             for j in range(1, h):
                 pass_copy(k, j).start()
@@ -166,8 +168,9 @@
         head = pack(x[t, 0].astype(jnp.float32), 0, t, head)
     send[0, 0:HEAD, :] = head.astype(jnp.bfloat16)
     pl.semaphore_wait(barrier, n - 1)
-    pump(min(WINDOW, 2 * rows))
+    pump(WINDOW)
     load_rest.wait()
+    relay(1)
 
     def first_diagonal(i, head):
         total = mm(x[i, 0], x[i, 0], NT)
@@ -187,10 +190,11 @@
         if t == 0:
             head = lax.fori_loop(0, rows, first_diagonal, jnp.zeros((HEAD, half_tile), jnp.float32))
             send[1, 0:HEAD, :] = head.astype(jnp.bfloat16)
+            limit[0] = pieces
+            relay(2)
+            lax.fori_loop(0, rows, first_local, 0, unroll=True)
         arrive(2 * t)
         arrive(2 * t + 1)
-        if t == 0:
-            lax.fori_loop(0, rows, first_local, 0, unroll=True)
         unpack(0, t)
         todo = ready(t)
 

time: 41.8 us -> 43.6 us (1.043)
  Pallas kernels: 41 us -> 42.8 us
    pallas_call x1, Pallas kernels: 37.1 us -> 38.9 us  [shards(): pl.pallas_call(functools.partial(purify_kernel, n), out_shape=(pltpu.VMEM...]
where the time goes in v1:
time: 43.6 us; the launch traced here: 43.4 us
  Pallas kernels  42.8 us (98%)
  between operations  0.64 us (1%)
    pallas_call x1, Pallas kernels, shards(): pl.pallas_call(functools.partial(purify_kernel, n), out_shape=(pltpu.VMEM...  38.9 us
    pallas_call x1, Pallas kernels, shards(): pl.pallas_call(write_kernel, out_shape=(jax.ShapeDtypeStruct(x_tiles.shap...  3.93 us

profile of v1, /device:TPU:0, one launch (start us, length us, event | category | flops | bytes accessed | tf_op | source)
XLA Modules:
  0.0 43.4 jit_solution(664487608857484938)
XLA Ops:
  0.6 38.9 %purify.1 = (f32[4,8,256,256]{3,2,1,0:T(8,128)S(1)}, f32[8,128]{1,0:T(8,128)S(1)}) custom-call(s32[4,8]{1,0:T(4,128)} %cols_hbm.1, s32[1,2]{1,0:T(1,128)} %branch_hbm.1, bf16[4,8,256,256]{3,2,1,0:T(8,128)(2,1)} %x_hbm.1), custom_call_target="tpu_custom_call" | custom-call | flops 5905580032 | bytes 12582912 | tf_op jit(solution)/shard_map/purify/pallas_call | solution.py:307
  39.5 3.9 %write.1 = (f32[4,8,256,256]{3,2,1,0:T(8,128)}, f32[1]{0:T(128)}) custom-call(f32[4,8,256,256]{3,2,1,0:T(8,128)S(1)} %get-tuple-element.4.held, f32[8,128]{1,0:T(8,128)S(1)} %get-tuple-element.5.occ_ref), custom_call_target="tpu_custom_call" | custom-call | bytes 8388608 | tf_op jit(solution)/shard_map/write/pallas_call | solution.py:337

commit v2 on v1

--- a/solution.py
+++ b/solution.py
@@ -9,7 +9,7 @@
 
 MESH = pl.DeviceIdType.MESH
 HEAD = 16
-WINDOW = 8
+WINDOW = 3
 AHEAD = 2
 NN = (((1,), (0,)), ((), ()))
 NT = (((1,), (1,)), ((), ()))
@@ -19,14 +19,23 @@
     return lax.dot_general(a, b, dims, preferred_element_type=jnp.float32)
 
 
+def ready(rows, slots, t):
+    return [s for s in range(slots - 1) if max(s % rows, (s + 1) % rows) == t]
+
+
+def chosen(cols_ref, gath, i, s, half_rows):
+    return lax.select(lax.rem(cols_ref[i, s + 1], half_rows) == s, gath[s], gath[s + 1])
+
+
 def purify_kernel(
-    n, cols_hbm, branch_hbm, x_hbm, out_ref, occ_ref,
-    cols_ref, branch_ref, x, d1, send, recv, gath, trace, load_sem, send_sem, recv_sem, pass_sem, tsend_sem, trecv_sem,
+    n, cols_hbm, branch_hbm, x_hbm, out_ref, occ_ref, d1, gath_last,
+    cols_ref, branch_ref, x, send, recv, gath_first, trace, load_sem, send_sem, recv_sem, pass_sem, tsend_sem, trecv_sem,
 ):
     rows, slots, size = x.shape[0], x.shape[1], x.shape[2]
     half_tile = size // 2
     h = n // 2
     half_rows = rows * h
+    gath = (gath_first, gath_last)
     me = lax.axis_index("col")
     upper = (me >= h).astype(jnp.int32)
     mine = me - upper * h
@@ -147,20 +156,13 @@
             a11 = jnp.where(ri <= ci, mixed, turned)
             a22 = jnp.where(ri > ci, mixed, jnp.where(ri == ci, corner, turned))
             g = r * rows + t
-            gath[step, g, 0:half_tile, 0:half_tile] = a11.astype(jnp.bfloat16)
-            gath[step, g, half_tile:, half_tile:] = a22.astype(jnp.bfloat16)
-            gath[step, g, 0:half_tile, half_tile:] = cross
-            gath[step, g, half_tile:, 0:half_tile] = cross.astype(jnp.float32).T.astype(jnp.bfloat16)
-
-    def ready(t):
-        return [
-            s for s in range(slots - 1)
-            if max(s % rows, (s + 1) % rows) == t
-        ]
+            gath[step][g, 0:half_tile, 0:half_tile] = a11.astype(jnp.bfloat16)
+            gath[step][g, half_tile:, half_tile:] = a22.astype(jnp.bfloat16)
+            gath[step][g, 0:half_tile, half_tile:] = cross
+            gath[step][g, half_tile:, 0:half_tile] = cross.astype(jnp.float32).T.astype(jnp.bfloat16)
 
     def other(step, i, s):
-        first = lax.rem(cols_ref[i, s + 1], half_rows) == s
-        return lax.select(first, gath[step, s], gath[step, s + 1])
+        return chosen(cols_ref, gath[step], i, s, half_rows)
 
     load_diag.wait()
     head = jnp.zeros((HEAD, half_tile), jnp.float32)
@@ -170,7 +172,6 @@
     pl.semaphore_wait(barrier, n - 1)
     pump(WINDOW)
     load_rest.wait()
-    relay(1)
 
     def first_diagonal(i, head):
         total = mm(x[i, 0], x[i, 0], NT)
@@ -196,7 +197,7 @@
         arrive(2 * t)
         arrive(2 * t + 1)
         unpack(0, t)
-        todo = ready(t)
+        todo = ready(rows, slots, t)
 
         def first_partner(i, carry):
             for s in todo:
@@ -254,14 +255,14 @@
             arrive(2 * (rows + t))
             arrive(2 * (rows + t) + 1)
             unpack(1, t)
-        todo = ready(t)
+        todo = ready(rows, slots, t)
 
         def second_partner(i, carry):
             for s in todo:
                 out_ref[i, s + 1] = out_ref[i, s + 1] + signs[1] * mm(d1[i, s + 1], other(1, i, s))
             return carry
 
-        if todo:
+        if todo and t < rows - 1:
             lax.fori_loop(0, rows, second_partner, 0, unroll=True)
 
     for k in range(1, n):
@@ -281,45 +282,62 @@
             pass_copy(k, j).wait_send()
 
 
-def write_kernel(held, occ_ref, out_hbm, occ_out, sem):
+def write_kernel(cols_hbm, branch_hbm, held, occ_ref, d1, gath, out_hbm, occ_out, cols_ref, branch_ref, fresh, load_sem, sem):
     rows, slots = held.shape[0], held.shape[1]
+    half_rows = gath.shape[0]
+    todo = ready(rows, slots, rows - 1)
+    load_cols = pltpu.make_async_copy(cols_hbm, cols_ref, load_sem.at[0])
+    load_branch = pltpu.make_async_copy(branch_hbm, branch_ref, load_sem.at[1])
+    load_cols.start()
+    load_branch.start()
 
     def part(i, j):
-        span = pl.ds(2 * j, 2)
-        return pltpu.make_async_copy(held.at[i, span], out_hbm.at[i, span], sem.at[i, j])
+        source = fresh.at[i, todo.index(j - 1)] if j - 1 in todo else held.at[i, j]
+        return pltpu.make_async_copy(source, out_hbm.at[i, j], sem.at[i, j])
 
     for i in range(rows):
-        for j in range(slots // 2):
-            part(i, j).start()
+        for j in range(slots):
+            if j - 1 not in todo:
+                part(i, j).start()
     occ_out[...] = occ_ref[0, 0:1]
+    load_cols.wait()
+    load_branch.wait()
+    sign = (2 * branch_ref[0, 1] - 1).astype(jnp.float32)
     for i in range(rows):
-        for j in range(slots // 2):
+        for at, s in enumerate(todo):
+            partner = mm(d1[i, s + 1], chosen(cols_ref, gath, i, s, half_rows))
+            fresh[i, at] = held[i, s + 1] + sign * partner
+            part(i, s + 1).start()
+    for i in range(rows):
+        for j in range(slots):
             part(i, j).wait()
 
 
 def shards(n, x_tiles, columns, branch):
     rows, slots, size = x_tiles.shape[0], x_tiles.shape[1], x_tiles.shape[2]
     h = n // 2
+    last = len(ready(rows, slots, rows - 1))
     length = HEAD + rows * size
     vmem = pl.BlockSpec(memory_space=pltpu.VMEM)
     hbm = pl.BlockSpec(memory_space=pltpu.HBM)
     flops = 2 * size**3 * rows * (slots * 2 + (slots - 1) * 4)
-    held, occ = pl.pallas_call(
+    held, occ, low, gath = pl.pallas_call(
         functools.partial(purify_kernel, n),
         out_shape=(
             pltpu.VMEM(x_tiles.shape, jnp.float32),
             pltpu.VMEM((8, 128), jnp.float32),
+            pltpu.VMEM(x_tiles.shape, jnp.bfloat16),
+            pltpu.VMEM((h * rows, size, size), jnp.bfloat16),
         ),
         in_specs=[hbm, hbm, hbm],
-        out_specs=(vmem, vmem),
+        out_specs=(vmem, vmem, vmem, vmem),
         scratch_shapes=[
             pltpu.SMEM(columns.shape, jnp.int32),
             pltpu.SMEM(branch.shape, jnp.int32),
             pltpu.VMEM((rows, slots, size, size), jnp.bfloat16),
-            pltpu.VMEM((rows, slots, size, size), jnp.bfloat16),
             pltpu.VMEM((2, length, size // 2), jnp.bfloat16),
             pltpu.VMEM((2, h, length, size // 2), jnp.bfloat16),
-            pltpu.VMEM((2, h * rows, size, size), jnp.bfloat16),
+            pltpu.VMEM((h * rows, size, size), jnp.bfloat16),
             pltpu.VMEM((n, 8, size // 2), jnp.float32),
             pltpu.SemaphoreType.DMA((4,)),
             pltpu.SemaphoreType.DMA((2, 2 * rows)),
@@ -329,7 +347,7 @@
             pltpu.SemaphoreType.DMA((n,)),
         ],
         compiler_params=pltpu.CompilerParams(
-            collective_id=0, has_side_effects=True, vmem_limit_bytes=40 * 2**20
+            collective_id=0, has_side_effects=True, vmem_limit_bytes=32 * 2**20
         ),
         cost_estimate=pl.CostEstimate(flops=flops, bytes_accessed=3 * x_tiles.size * 2, transcendentals=0),
         name="purify",
@@ -340,15 +358,22 @@
             jax.ShapeDtypeStruct(x_tiles.shape, jnp.float32),
             jax.ShapeDtypeStruct((1,), jnp.float32),
         ),
-        in_specs=[vmem, vmem],
+        in_specs=[hbm, hbm, vmem, vmem, vmem, vmem],
         out_specs=(hbm, vmem),
-        scratch_shapes=[pltpu.SemaphoreType.DMA((rows, slots // 2))],
-        compiler_params=pltpu.CompilerParams(vmem_limit_bytes=4 * 2**20),
+        scratch_shapes=[
+            pltpu.SMEM(columns.shape, jnp.int32),
+            pltpu.SMEM(branch.shape, jnp.int32),
+            pltpu.VMEM((rows, last, size, size), jnp.float32),
+            pltpu.SemaphoreType.DMA((2,)),
+            pltpu.SemaphoreType.DMA((rows, slots)),
+        ],
+        compiler_params=pltpu.CompilerParams(vmem_limit_bytes=12 * 2**20),
         cost_estimate=pl.CostEstimate(flops=0, bytes_accessed=x_tiles.size * 4, transcendentals=0),
         name="write",
     )(
-        pltpu.with_memory_space_constraint(held, pltpu.VMEM),
-        pltpu.with_memory_space_constraint(occ, pltpu.VMEM),
+        pltpu.with_memory_space_constraint(columns, pltpu.HBM),
+        pltpu.with_memory_space_constraint(branch, pltpu.HBM),
+        *[pltpu.with_memory_space_constraint(a, pltpu.VMEM) for a in (held, occ, low, gath)],
     )
 
 

time: 43.6 us -> 41.4 us (0.950)
  Pallas kernels: 42.8 us -> 40.6 us
    pallas_call x1, Pallas kernels: 38.9 us -> 36.6 us  [shards(): pl.pallas_call(functools.partial(purify_kernel, n), out_shape=(pltpu.VMEM...]
where the time goes in v2:
time: 41.4 us; the launch traced here: 41.3 us
  Pallas kernels  40.6 us (98%)
  between operations  0.64 us (2%)
    pallas_call x1, Pallas kernels, shards(): pl.pallas_call(functools.partial(purify_kernel, n), out_shape=(pltpu.VMEM...  36.6 us
    pallas_call x1, Pallas kernels, shards(): pl.pallas_call(write_kernel, out_shape=(jax.ShapeDtypeStruct(x_tiles.shap...  4.07 us

profile of v2, /device:TPU:0, one launch (start us, length us, event | category | flops | bytes accessed | tf_op | source)
XLA Modules:
  0.0 41.3 jit_solution(1515180086645944825)
XLA Ops:
  0.6 36.6 %purify.1 = (f32[4,8,256,256]{3,2,1,0:T(8,128)S(1)}, f32[8,128]{1,0:T(8,128)S(1)}, bf16[4,8,256,256]{3,2,1,0:T(8,128)(2,1)S(1)}, bf16[8,256,256]{2,1,0:T(8,128)(2,1)S(1)}) custom-call(s32[4,8]{1,0:T(4,128)} %cols_hbm.3, s32[1,2]{1,0:T(1,128)} %branch_hbm.3, bf16[4,8,256,256]{3,2,1,0:T(8,128)(2,1)} %x_hbm.1), custom_call_target="tpu_custom_call" | custom-call | flops 5905580032 | bytes 12582912 | tf_op jit(solution)/shard_map/purify/pallas_call | solution.py:324
  37.2 4.1 %write.1 = (f32[4,8,256,256]{3,2,1,0:T(8,128)}, f32[1]{0:T(128)}) custom-call(s32[4,8]{1,0:T(4,128)} %cols_hbm.3, s32[1,2]{1,0:T(1,128)} %branch_hbm.3, f32[4,8,256,256]{3,2,1,0:T(8,128)S(1)} %get-tuple-element.6.held, f32[8,128]{1,0:T(8,128)S(1)} %get-tuple-element.7.occ_ref, bf16[4,8,256,256]{3,2,1,0:T(8,128)(2,1)S(1)} %get-tuple-element.8.d1, ...), custom_call_target="tpu_custom_call" | custom-call | bytes 8388608 | tf_op jit(solution)/shard_map/write/pallas_call | solution.py:355

commit v3 on v2

--- a/solution.py
+++ b/solution.py
@@ -9,7 +9,7 @@
 
 MESH = pl.DeviceIdType.MESH
 HEAD = 16
-WINDOW = 3
+WINDOW = 2
 AHEAD = 2
 NN = (((1,), (0,)), ((), ()))
 NT = (((1,), (1,)), ((), ()))
@@ -223,7 +223,12 @@
         on_diag = jnp.where(eye, new, 0.0)
         return carry + jnp.sum(jnp.sum(on_diag.reshape(size // 8, 8, 2, half_tile), axis=0), axis=1)
 
-    lanes = lax.fori_loop(0, rows, second_diagonal, jnp.zeros((8, half_tile), jnp.float32))
+    lanes = jnp.zeros((8, half_tile), jnp.float32)
+    middle = rows // 2
+    if middle:
+        lanes = lax.fori_loop(0, middle, second_diagonal, lanes)
+        relay(direct[0] + 1)
+    lanes = lax.fori_loop(middle, rows, second_diagonal, lanes)
     trace[me] = lanes
 
     def trace_copy(k):

time: 41.4 us -> 41.4 us (level)
  no operation moved by 1% of the time
where the time goes in v3:
time: 41.4 us; the launch traced here: 41.3 us
  Pallas kernels  40.6 us (98%)
  between operations  0.64 us (2%)
    pallas_call x1, Pallas kernels, shards(): pl.pallas_call(functools.partial(purify_kernel, n), out_shape=(pltpu.VMEM...  36.5 us
    pallas_call x1, Pallas kernels, shards(): pl.pallas_call(write_kernel, out_shape=(jax.ShapeDtypeStruct(x_tiles.shap...  4.07 us

profile of v3, /device:TPU:0, one launch (start us, length us, event | category | flops | bytes accessed | tf_op | source)
XLA Modules:
  0.0 41.3 jit_solution(8327628310466985552)
XLA Ops:
  0.6 36.5 %purify.1 = (f32[4,8,256,256]{3,2,1,0:T(8,128)S(1)}, f32[8,128]{1,0:T(8,128)S(1)}, bf16[4,8,256,256]{3,2,1,0:T(8,128)(2,1)S(1)}, bf16[8,256,256]{2,1,0:T(8,128)(2,1)S(1)}) custom-call(s32[4,8]{1,0:T(4,128)} %cols_hbm.3, s32[1,2]{1,0:T(1,128)} %branch_hbm.3, bf16[4,8,256,256]{3,2,1,0:T(8,128)(2,1)} %x_hbm.1), custom_call_target="tpu_custom_call" | custom-call | flops 5905580032 | bytes 12582912 | tf_op jit(solution)/shard_map/purify/pallas_call | solution.py:329
  37.2 4.1 %write.1 = (f32[4,8,256,256]{3,2,1,0:T(8,128)}, f32[1]{0:T(128)}) custom-call(s32[4,8]{1,0:T(4,128)} %cols_hbm.3, s32[1,2]{1,0:T(1,128)} %branch_hbm.3, f32[4,8,256,256]{3,2,1,0:T(8,128)S(1)} %get-tuple-element.6.held, f32[8,128]{1,0:T(8,128)S(1)} %get-tuple-element.7.occ_ref, bf16[4,8,256,256]{3,2,1,0:T(8,128)(2,1)S(1)} %get-tuple-element.8.d1, ...), custom_call_target="tpu_custom_call" | custom-call | bytes 8388608 | tf_op jit(solution)/shard_map/write/pallas_call | solution.py:360
